TPU v7x, 32 devices: a whole 2x2x4 slice. The times are simulated.
32 devices in a mesh: groups: 2 (over x), gx: 16 (over z, y, core).
Axes of the slice: x: 2, y: 2, z: 4, core: 2. Of those that a mesh axis runs over, the one named last changes fastest.
Arguments:
- fine_in: float32 [48, 64, 16, 32], P(None, ('groups', 'gx')), parts along dimension 1, may hold values from -6 to 6
- coarse_in: float32 [96, 32, 8, 16], P(None, ('groups', 'gx')), parts along dimension 1, may hold values from -6 to 6
- fine_wa: float32 [48, 48, 3, 3, 3], replicated, may hold values from -0.15625 to 0.15625
- fine_ba: float32 [48], replicated, may hold values from -3 to 3
- fine_wb: float32 [48, 48, 3, 3, 3], replicated, may hold values from -0.15625 to 0.15625
- fine_bb: float32 [48], replicated, may hold values from -3 to 3
- coarse_wa: float32 [96, 96, 3, 3, 3], replicated, may hold values from -0.125 to 0.125
- coarse_ba: float32 [96], replicated, may hold values from -3 to 3
- coarse_wb: float32 [96, 96, 3, 3, 3], replicated, may hold values from -0.125 to 0.125
- coarse_bb: float32 [96], replicated, may hold values from -3 to 3
- down_w: float32 [96, 48, 3, 3, 3], replicated, may hold values from -0.15625 to 0.15625
- down_b: float32 [96], replicated, may hold values from -3 to 3
- up_w: float32 [48, 96], replicated, may hold values from -0.625 to 0.625
- up_b: float32 [48], replicated, may hold values from -3 to 3
Outputs:
- fine_out: float32 [48, 64, 16, 32], P(None, ('groups', 'gx')), parts along dimension 1
- coarse_out: float32 [96, 32, 8, 16], P(None, ('groups', 'gx')), parts along dimension 1
There are 2 independent parts, one for each index of `groups`. A program takes and returns all parts, laid end to end along the dimension named above; an argument that names none is the same for every part. Nothing has to cross between parts.
All inputs are finite; a program needn't handle non-finite values.
Results may differ from a plain program's by a relative error of at most 0.000058.
Values sent between devices are 32-bit elements; how exact they have to be, the bound alone decides.
A program may use at most 128 MiB of HBM per device.

v0:
```python
import functools

import jax
import jax.numpy as jnp
from jax import lax
from jax.experimental import pallas as pl
from jax.experimental.pallas import tpu as pltpu
from jax.sharding import PartitionSpec as P

ROWS = 512


def halves(value):
    high = value.astype(jnp.bfloat16)
    return high, (value - high.astype(jnp.float32)).astype(jnp.bfloat16)


def put_patches(value, high_ref, low_ref, slot, width, base=None):
    rows, channels = value.shape
    place = lax.rem(lax.broadcasted_iota(jnp.int32, (rows, channels), 0), width)
    before = jnp.where(place == 0, 0.0, pltpu.roll(value, 1, 0))
    after = jnp.where(place == width - 1, 0.0, pltpu.roll(value, rows - 1, 0))
    for k, part in enumerate((before, value, after)):
        high, low = halves(part)
        at = pl.ds(k * channels, channels)
        high_ref[slot, pl.ds(width, rows), at] = high
        low_ref[slot, pl.ds(width, rows), at] = low


def clear_rims(high_ref, low_ref, width):
    slots, rows, lanes = high_ref.shape
    zero = jnp.zeros((slots, width, lanes), jnp.bfloat16)
    for ref in (high_ref, low_ref):
        ref[:, pl.ds(0, width), :] = zero
        ref[:, pl.ds(rows - width, width), :] = zero


def product(high, low, weights):
    out = weights.shape[1] // 2
    both = jnp.dot(high, weights, preferred_element_type=jnp.float32)
    third = jnp.dot(low, weights[:, :out], preferred_element_type=jnp.float32)
    return both[:, :out] + both[:, out:] + third


def conv_chunk(high_ref, low_ref, w_ref, slot, start, rows, width):
    total = None
    for p in range(3):
        for q in range(3):
            at = pl.ds(pl.multiple_of(start + q * width, 16), rows)
            term = product(high_ref[slot + p, at, :], low_ref[slot + p, at, :], w_ref[3 * p + q])
            total = term if total is None else total + term
    return total


def conv_plane(high_ref, low_ref, w_ref, temp_ref, slot, width, finish):
    rows = temp_ref.shape[0]
    step = min(ROWS, rows)

    def body(i, _):
        start = i * step
        at = pl.ds(pl.multiple_of(start, 16), step)
        temp_ref[at, :] = finish(
            conv_chunk(high_ref, low_ref, w_ref, slot, start, step, width), at
        )
        return 0

    if rows == step:
        temp_ref[...] = finish(
            conv_chunk(high_ref, low_ref, w_ref, slot, 0, step, width), pl.ds(0, step)
        )
    else:
        lax.fori_loop(0, rows // step, body, 0)


def compute(
    count, width, narrow,
    f7, c5, wfa, bfa, wfb, bfb, wca, bca, wcb, bcb, wd, bd, wu, bu,
    fine_ref, coarse_ref, moved_ref, projected_ref,
    fhi, flo, chi, clo, ftemp, ctemp, mtemp, *staged,
):
    me = lax.axis_index("gx")

    def plane_of(j):
        if not staged:
            return f7.at[j]
        copy = pltpu.make_async_copy(f7.at[j], staged[0], staged[1])
        copy.start()
        copy.wait()
        return staged[0]

    clear_rims(chi, clo, narrow)

    def coarse_load(j, _):
        put_patches(c5[j], chi, clo, j, narrow)
        return 0

    lax.fori_loop(0, 5, coarse_load, 0)

    def coarse_mid(j, _):
        y = me - 1 + j
        inside = jnp.where((y >= 0) & (y < count), 1.0, 0.0)
        conv_plane(
            chi, clo, wca, ctemp, j, narrow,
            lambda total, at: jnp.maximum(total + bca[...], 0.0) * inside,
        )
        put_patches(ctemp[...], chi, clo, j, narrow)
        return 0

    lax.fori_loop(0, 3, coarse_mid, 0)
    conv_plane(
        chi, clo, wcb, ctemp, 0, narrow,
        lambda total, at: jnp.maximum(c5[2, at, :] + total + bcb[...], 0.0),
    )
    coarse = ctemp[...]
    coarse_ref[...] = coarse
    projected_ref[...] = product(*halves(coarse), wu[...]) + bu[...]

    clear_rims(fhi, flo, width)

    def fine_load(j, _):
        put_patches(plane_of(j)[...], fhi, flo, j, width)
        return 0

    lax.fori_loop(0, 7, fine_load, 0)

    def fine_mid(j, _):
        x = 2 * me - 2 + j
        inside = jnp.where((x >= 0) & (x < 2 * count), 1.0, 0.0)
        conv_plane(
            fhi, flo, wfa, ftemp, j, width,
            lambda total, at: jnp.maximum(total + bfa[...], 0.0) * inside,
        )
        put_patches(ftemp[...], fhi, flo, j, width)
        return 0

    lax.fori_loop(0, 5, fine_mid, 0)

    def fine_last(j, _):
        x = 2 * me - 1 + j
        inside = jnp.where(x >= 0, 1.0, 0.0)
        own = plane_of(j + 2)
        conv_plane(
            fhi, flo, wfb, ftemp, j, width,
            lambda total, at: jnp.maximum(own[at, :] + total + bfb[...], 0.0) * inside,
        )
        fine = ftemp[...]
        put_patches(fine, fhi, flo, j, width)
        fine_ref[jnp.maximum(j - 1, 0)] = fine
        return 0

    lax.fori_loop(0, 3, fine_last, 0)

    levels = moved_ref.shape[0] // narrow
    some = max(1, min(levels, ROWS // width))
    for first in range(0, levels, some):
        total = None
        for p in range(3):
            for q in range(3):
                def rows_of(ref):
                    return jnp.concatenate(
                        [ref[p, pl.ds((2 * b + q) * width, width), :] for b in range(first, first + some)],
                        axis=0,
                    )
                term = product(rows_of(fhi), rows_of(flo), wd[3 * p + q])
                total = term if total is None else total + term
        channels = total.shape[1]
        mtemp[:, pl.ds(0, channels)] = total + bd[...]
        moved_ref[pl.ds(first * narrow, some * narrow), :] = mtemp[
            pl.ds(0, some * narrow, stride=2), :
        ][:, :channels]


def split_weights(w):
    out, inner = w.shape[:2]
    moved = jnp.transpose(w, (2, 3, 4, 1, 0)).reshape(9, 3 * inner, out)
    high = lax.reduce_precision(moved, 8, 7)
    return jnp.concatenate([high, moved - high], axis=2).astype(jnp.bfloat16)


def shifted(value, steps):
    count = lax.axis_size("gx")
    pairs = [(i, i + steps) for i in range(count) if 0 <= i + steps < count]
    return lax.ppermute(value, "gx", pairs)


def per_device(
    fine_in, coarse_in,
    fine_wa, fine_ba, fine_wb, fine_bb,
    coarse_wa, coarse_ba, coarse_wb, coarse_bb,
    down_w, down_b, up_w, up_b,
):
    count = lax.axis_size("gx")
    cf, planes, depth, width = fine_in.shape
    cc, _, levels, narrow = coarse_in.shape
    own = jnp.transpose(fine_in, (1, 2, 3, 0)).reshape(planes, depth * width, cf)
    slab = jnp.transpose(coarse_in, (1, 2, 3, 0)).reshape(1, levels * narrow, cc)
    f7 = jnp.concatenate(
        [shifted(own[1:], 2), shifted(own, 1), own, shifted(own, -1)], axis=0
    )
    c5 = jnp.concatenate(
        [shifted(slab, 2), shifted(slab, 1), slab, shifted(slab, -1), shifted(slab, -2)], axis=0
    )
    up = up_w.T
    up_high = lax.reduce_precision(up, 8, 7)
    wu = jnp.concatenate([up_high, up - up_high], axis=1).astype(jnp.bfloat16)
    frows, crows = depth * width, levels * narrow
    some = max(1, min(levels, ROWS // width))
    vmem = pl.BlockSpec(memory_space=pltpu.VMEM)
    large = frows > 1024
    stage = [pltpu.VMEM((frows, cf), jnp.float32), pltpu.SemaphoreType.DMA] if large else []
    fine, coarse, moved, projected = pl.pallas_call(
        functools.partial(compute, count, width, narrow),
        out_shape=(
            jax.ShapeDtypeStruct((planes, frows, cf), jnp.float32),
            jax.ShapeDtypeStruct((crows, cc), jnp.float32),
            jax.ShapeDtypeStruct((crows, cc), jnp.float32),
            jax.ShapeDtypeStruct((crows, cf), jnp.float32),
        ),
        in_specs=[pl.BlockSpec(memory_space=pl.ANY) if large else vmem] + [vmem] * 13,
        out_specs=(vmem,) * 4,
        scratch_shapes=[
            pltpu.VMEM((7, frows + 2 * width, 3 * cf), jnp.bfloat16),
            pltpu.VMEM((7, frows + 2 * width, 3 * cf), jnp.bfloat16),
            pltpu.VMEM((5, crows + 2 * narrow, 3 * cc), jnp.bfloat16),
            pltpu.VMEM((5, crows + 2 * narrow, 3 * cc), jnp.bfloat16),
            pltpu.VMEM((frows, cf), jnp.float32),
            pltpu.VMEM((crows, cc), jnp.float32),
            pltpu.VMEM((some * width, 128), jnp.float32),
        ] + stage,
        compiler_params=pltpu.CompilerParams(vmem_limit_bytes=(60 if large else 30) * 2**20),
        cost_estimate=pl.CostEstimate(flops=10**9, bytes_accessed=6 * 10**6, transcendentals=0),
    )(
        f7, c5,
        split_weights(fine_wa), fine_ba[None], split_weights(fine_wb), fine_bb[None],
        split_weights(coarse_wa), coarse_ba[None], split_weights(coarse_wb), coarse_bb[None],
        split_weights(down_w), down_b[None], wu, up_b[None],
    )
    both = jnp.concatenate(
        [
            jnp.transpose(moved.reshape(levels, narrow, cc), (1, 0, 2)),
            jnp.transpose(projected.reshape(levels, narrow, cf), (1, 0, 2)),
        ],
        axis=2,
    )
    arrived = lax.all_to_all(both, "gx", split_axis=0, concat_axis=0, tiled=True)
    reduced = jnp.transpose(arrived[:, :, :cc], (1, 0, 2))
    raised = jnp.transpose(arrived[:, :, cc:], (1, 0, 2))
    coarse_out = jax.nn.gelu(coarse.reshape(levels, narrow, cc) + reduced, approximate=False)
    raised = jnp.broadcast_to(
        raised[None, :, None, :, None, :], (planes, levels, depth // levels, narrow, width // narrow, cf)
    ).reshape(planes, depth, width, cf)
    fine_out = jax.nn.gelu(fine.reshape(planes, depth, width, cf) + raised, approximate=False)
    return (
        jnp.transpose(fine_out, (3, 0, 1, 2)),
        jnp.transpose(coarse_out, (2, 0, 1))[:, None],
    )


def solution(mesh):
    split = P(None, ("groups", "gx"), None, None)
    return jax.shard_map(
        per_device,
        mesh=mesh,
        in_specs=(split, split) + (P(),) * 12,
        out_specs=(split, split),
        check_vma=False,
    )
```

profile of v0, /device:TPU:0, one launch (start us, length us, event | category | flops | bytes accessed | tf_op | source)
XLA Modules:
  0.0 90.3 jit_solution(1549819362547907292)
XLA Ops:
  0.6 5.5 %collective-permute-start.3 = (f32[1,128,96]{2,1,0:T(8,128)}, f32[1,128,96]{2,1,0:T(8,128)}, u32[]{:S(2)}, u32[]{:S(2)}) collective-permute-start(f32[1,128,96]{2,1,0:T(8,128)} %bitcast.77), channel_id=1, source_target_pairs={{0,2},{1,3},{2,4},{3,5},{4,6},{5,7},{6,8},{7,9},{8,10},{9,11},{10,... | collective-permute-start | bytes 147464 | tf_op jit(solution)/shard_map/ppermute | solution.py:183
  6.1 2.1 %collective-permute-start.4 = (f32[1,128,96]{2,1,0:T(8,128)}, f32[1,128,96]{2,1,0:T(8,128)}, u32[]{:S(2)}, u32[]{:S(2)}) collective-permute-start(f32[1,128,96]{2,1,0:T(8,128)} %bitcast.78), channel_id=1, source_target_pairs={{0,1},{1,2},{2,3},{3,4},{4,5},{5,6},{6,7},{7,8},{8,9},{9,10},{10,1... | collective-permute-start | bytes 147464 | tf_op jit(solution)/shard_map/ppermute | solution.py:183
  8.2 1.3 %collective-permute-start.5 = (f32[1,128,96]{2,1,0:T(8,128)}, f32[1,128,96]{2,1,0:T(8,128)}, u32[]{:S(2)}, u32[]{:S(2)}) collective-permute-start(f32[1,128,96]{2,1,0:T(8,128)} %bitcast.79), channel_id=1, source_target_pairs={{1,0},{2,1},{3,2},{4,3},{5,4},{6,5},{7,6},{8,7},{9,8},{10,9},{11,1... | collective-permute-start | bytes 147464 | tf_op jit(solution)/shard_map/ppermute | solution.py:183
  9.5 1.3 %collective-permute-start.6 = (f32[1,128,96]{2,1,0:T(8,128)}, f32[1,128,96]{2,1,0:T(8,128)}, u32[]{:S(2)}, u32[]{:S(2)}) collective-permute-start(f32[1,128,96]{2,1,0:T(8,128)} %bitcast.80), channel_id=1, source_target_pairs={{2,0},{3,1},{4,2},{5,3},{6,4},{7,5},{8,6},{9,7},{10,8},{11,9},{12,... | collective-permute-start | bytes 147464 | tf_op jit(solution)/shard_map/ppermute | solution.py:183
  10.8 1.2 %copy.48 = f32[2,512,48]{1,2,0:T(8,128)S(1)} copy(f32[2,512,48]{2,1,0:T(8,128)} %bitcast.68) | data formatting | bytes 393216 | tf_op jit(solution)/shard_map/reshape | solution.py:195
  12.0 4.1 %collective-permute-start.1 = (f32[2,512,48]{1,2,0:T(8,128)S(1)}, f32[2,512,48]{1,2,0:T(8,128)}, u32[]{:S(2)}, u32[]{:S(2)}) collective-permute-start(f32[2,512,48]{1,2,0:T(8,128)S(1)} %copy.48), channel_id=1, source_target_pairs={{0,1},{1,2},{2,3},{3,4},{4,5},{5,6},{6,7},{7,8},{8,9},{9,10},{10,1... | collective-permute-start | bytes 589832 | tf_op jit(solution)/shard_map/ppermute | solution.py:183
  16.1 1.7 %copy.39 = f32[3,3,3,96,96]{4,3,2,1,0:T(8,128)S(1)} copy(f32[3,3,3,96,96]{3,4,2,1,0:T(8,128)} %bitcast.66) | data formatting | bytes 1990656 | tf_op jit(solution)/shard_map/transpose | solution.py:175
  18.1 1.7 %copy.38 = f32[3,3,3,96,96]{4,3,2,1,0:T(8,128)S(1)} copy(f32[3,3,3,96,96]{3,4,2,1,0:T(8,128)} %bitcast.67) | data formatting | bytes 1990656 | tf_op jit(solution)/shard_map/transpose | solution.py:175
  19.8 1.1 %reduce-precision_convert_fusion.1 = (bf16[9,288,96]{2,1,0:T(8,128)(2,1)S(1)}, bf16[9,288,96]{2,1,0:T(8,128)(2,1)}) fusion(f32[9,288,96]{2,1,0:T(8,128)S(1)} %bitcast.63), kind=kLoop, calls=%fused_computation.3 | loop fusion | flops 995328 | bytes 1990656 | tf_op jit(solution)/shard_map/convert.6
  20.9 1.4 %copy.37 = f32[3,3,3,48,48]{4,3,2,1,0:T(8,128)S(1)} copy(f32[3,3,3,48,48]{3,4,2,1,0:T(8,128)} %bitcast.72) | data formatting | bytes 497664 | tf_op jit(solution)/shard_map/transpose | solution.py:175
  22.3 0.9 %reduce-precision_convert_fusion.3 = (bf16[9,144,48]{2,1,0:T(8,128)(2,1)}, bf16[9,144,48]{2,1,0:T(8,128)(2,1)}) fusion(f32[9,144,48]{2,1,0:T(8,128)S(1)} %bitcast.64), kind=kLoop, calls=%fused_computation.11 | loop fusion | flops 248832 | bytes 497664 | tf_op jit(solution)/shard_map/convert.8
  23.5 0.9 %reduce-precision_convert_fusion.4 = (bf16[9,144,48]{2,1,0:T(8,128)(2,1)}, bf16[9,144,48]{2,1,0:T(8,128)(2,1)}) fusion(f32[9,144,48]{2,1,0:T(8,128)S(1)} %bitcast.65), kind=kLoop, calls=%fused_computation.13 | loop fusion | flops 248832 | bytes 497664 | tf_op jit(solution)/shard_map/convert.10
  24.9 1.1 %pad_maximum_fusion.3.wd = bf16[9,144,192]{2,1,0:T(8,128)(2,1)} fusion(bf16[9,144,96]{2,1,0:T(8,128)(2,1)S(1)} %get-tuple-element.19, bf16[9,144,96]{2,1,0:T(8,128)(2,1)S(1)} %get-tuple-element.18), kind=kLoop, calls=%fused_computation.19 | loop fusion | flops 995328 | bytes 995328 | tf_op jit(solution)/shard_map/concatenate | solution.py:177
  26.1 3.3 %pad_maximum_fusion = (bf16[9,288,192]{2,1,0:T(8,128)(2,1)S(1)}, bf16[9,288,192]{2,1,0:T(8,128)(2,1)}) fusion(bf16[9,288,96]{2,1,0:T(8,128)(2,1)} %get-tuple-element.17, bf16[9,288,96]{2,1,0:T(8,128)(2,1)S(1)} %get-tuple-element.16, bf16[9,288,96]{2,1,0:T(8,128)(2,1)S(1)} %get-tuple-element.15, bf16[9,288,96]{2,1,0:T(8,128)(2,1)S(1)} %get-tuple-element.14), kind=kLoop, calls=%fused_computation.6 | loop fusion | flops 3981312 | bytes 3981312 | tf_op jit(solution)/shard_map/concatenate | solution.py:177
  29.4 1.1 %pad_maximum_fusion.4 = (bf16[9,144,96]{2,1,0:T(8,128)(2,1)S(1)}, bf16[9,144,96]{2,1,0:T(8,128)(2,1)}) fusion(bf16[9,144,48]{2,1,0:T(8,128)(2,1)S(1)} %copy-done.14, bf16[9,144,48]{2,1,0:T(8,128)(2,1)S(1)} %copy-done.13, bf16[9,144,48]{2,1,0:T(8,128)(2,1)S(1)} %copy-done.12, bf16[9,144,48]{2,1,0:T(8,128)(2,1)S(1)} %copy-done.11), kind=kLoop, calls=%fused_computation.38 | loop fusion | flops 995328 | bytes 995328 | tf_op jit(solution)/shard_map/concatenate | solution.py:177
  30.8 1.3 %collective-permute-start.2 = (f32[2,512,48]{1,2,0:T(8,128)S(1)}, f32[2,512,48]{1,2,0:T(8,128)S(1)}, u32[]{:S(2)}, u32[]{:S(2)}) collective-permute-start(f32[2,512,48]{1,2,0:T(8,128)S(1)} %copy.48), channel_id=1, source_target_pairs={{1,0},{2,1},{3,2},{4,3},{5,4},{6,5},{7,6},{8,7},{9,8},{10,9},{11,1... | collective-permute-start | bytes 589832 | tf_op jit(solution)/shard_map/ppermute | solution.py:183
  32.1 0.8 constant_dynamic-update-slice_fusion.4
  32.9 5.8 %collective-permute-start = (f32[1,512,48]{1,2,0:T(8,128)S(1)}, f32[1,512,48]{1,2,0:T(8,128)S(1)}, u32[]{:S(2)}, u32[]{:S(2)}) collective-permute-start(f32[1,512,48]{1,2,0:T(8,128)S(1)} %copy.47), channel_id=1, source_target_pairs={{0,2},{1,3},{2,4},{3,5},{4,6},{5,7},{6,8},{7,9},{8,10},{9,11},{10,... | collective-permute-start | bytes 294920 | tf_op jit(solution)/shard_map/ppermute | solution.py:183
  38.8 0.8 constant_dynamic-update-slice_fusion.3
  39.6 0.8 constant_dynamic-update-slice_fusion.1
  40.5 0.8 constant_dynamic-update-slice_fusion.c5
  41.3 0.7 copy-done.3
  42.1 1.0 %collective-permute-done = f32[1,512,48]{1,2,0:T(8,128)S(1)} collective-permute-done((f32[1,512,48]{1,2,0:T(8,128)S(1)}, f32[1,512,48]{1,2,0:T(8,128)S(1)}, u32[]{:S(2)}, u32[]{:S(2)}) %collective-permute-start) | collective-permute-done | bytes 98336 | tf_op jit(solution)/shard_map/ppermute | solution.py:183
  43.0 1.8 %pad_maximum_fusion.2 = f32[7,512,48]{1,2,0:T(8,128)} fusion(f32[2,512,48]{1,2,0:T(8,128)S(1)} %collective-permute-done.2, f32[2,512,48]{1,2,0:T(8,128)S(1)} %copy.48, f32[2,512,48]{1,2,0:T(8,128)} %collective-permute-done.1, f32[1,512,48]{1,2,0:T(8,128)S(1)} %collective-permute-done), kind=kLoop, calls=%fused_computation.15 | loop fusion | flops 516096 | bytes 1376256 | tf_op jit(solution)/shard_map/concatenate | solution.py:197
  44.9 1.7 %copy.41.f7 = f32[7,512,48]{2,1,0:T(8,128)S(1)} copy(f32[7,512,48]{1,2,0:T(8,128)} %pad_maximum_fusion.2) | data formatting | bytes 1376256 | tf_op jit(solution)/shard_map/concatenate | solution.py:197
  46.7 1.3 %copy-done = bf16[9,288,192]{2,1,0:T(8,128)(2,1)S(1)} copy-done((bf16[9,288,192]{2,1,0:T(8,128)(2,1)S(1)}, bf16[9,288,192]{2,1,0:T(8,128)(2,1)}, u32[]{:S(2)}) %copy-start) | copy-done | bytes 995352
  48.0 1.1 %copy-done.1 = bf16[9,144,192]{2,1,0:T(8,128)(2,1)S(1)} copy-done((bf16[9,144,192]{2,1,0:T(8,128)(2,1)S(1)}, bf16[9,144,192]{2,1,0:T(8,128)(2,1)}, u32[]{:S(2)}) %copy-start.1) | copy-done | bytes 497688
  49.1 1.0 %copy-done.2 = bf16[9,144,96]{2,1,0:T(8,128)(2,1)S(1)} copy-done((bf16[9,144,96]{2,1,0:T(8,128)(2,1)S(1)}, bf16[9,144,96]{2,1,0:T(8,128)(2,1)}, u32[]{:S(2)}) %copy-start.2) | copy-done | bytes 248856
  50.1 1.0 %copy-done.4 = f32[5,128,96]{2,1,0:T(8,128)S(1)} copy-done((f32[5,128,96]{2,1,0:T(8,128)S(1)}, f32[5,128,96]{2,1,0:T(8,128)}, u32[]{:S(2)}) %copy-start.4) | copy-done | bytes 245784
  51.0 21.5 %shard_map.149 = (f32[2,512,48]{2,1,0:T(8,128)S(1)}, f32[128,96]{1,0:T(8,128)S(1)}, f32[128,96]{1,0:T(8,128)S(1)}, f32[128,48]{1,0:T(8,128)S(1)}) custom-call(f32[7,512,48]{2,1,0:T(8,128)S(1)} %copy.41.f7, f32[5,128,96]{2,1,0:T(8,128)S(1)} %copy-done.4, bf16[9,144,96]{2,1,0:T(8,128)(2,1)S(1)} %get-tuple-element.28.wfa, f32[1,48]{1,0:T(1,128)S(1)} %bitcast.56, ...), custom_call_target="tpu_custom_call" | custom-call | flops 1000000000 | bytes 6000000 | tf_op jit(solution)/shard_map/pallas_call | solution.py:211
  72.7 14.7 %all_to_all.5 = f32[16,8,144]{2,1,0:T(8,128)S(1)} all-to-all(f32[16,8,144]{2,1,0:T(8,128)S(1)} %pad_maximum_fusion.6), channel_id=1, replica_groups=mesh['groups'=2,'gx'=16] {'gx'}, dimensions={0} | all-to-all | bytes 147456 | tf_op jit(solution)/shard_map/all_to_all | solution.py:245
  88.4 1.9 %fusion.7 = f32[48,2,16,32]{0,3,2,1:T(8,128)} fusion(f32[2,16,32,48]{3,2,1,0:T(8,128)S(1)} %bitcast.52, f32[16,32,48]{2,1,0:T(8,128)S(1)} %bitcast.70), kind=kLoop, calls=%fused_computation.22 | loop fusion | flops 3194880 | bytes 491520 | tf_op jit(solution)/shard_map/transpose | solution.py:254
  (58 shorter events, 2.4 us)
Async XLA Ops:
  0.6 30.1 %collective-permute-start.3 = (f32[1,128,96]{2,1,0:T(8,128)}, f32[1,128,96]{2,1,0:T(8,128)}, u32[]{:S(2)}, u32[]{:S(2)}) collective-permute-start(f32[1,128,96]{2,1,0:T(8,128)} %bitcast.77), channel_id=1, source_target_pairs={{0,2},{1,3},{2,4},{3,5},{4,6},{5,7},{6,8},{7,9},{8,10},{9,11},{10,... | collective-permute-start | bytes 147464 | tf_op jit(solution)/shard_map/ppermute | solution.py:183
  6.1 26.8 %collective-permute-start.4 = (f32[1,128,96]{2,1,0:T(8,128)}, f32[1,128,96]{2,1,0:T(8,128)}, u32[]{:S(2)}, u32[]{:S(2)}) collective-permute-start(f32[1,128,96]{2,1,0:T(8,128)} %bitcast.78), channel_id=1, source_target_pairs={{0,1},{1,2},{2,3},{3,4},{4,5},{5,6},{6,7},{7,8},{8,9},{9,10},{10,1... | collective-permute-start | bytes 147464 | tf_op jit(solution)/shard_map/ppermute | solution.py:183
  8.2 31.4 %collective-permute-start.5 = (f32[1,128,96]{2,1,0:T(8,128)}, f32[1,128,96]{2,1,0:T(8,128)}, u32[]{:S(2)}, u32[]{:S(2)}) collective-permute-start(f32[1,128,96]{2,1,0:T(8,128)} %bitcast.79), channel_id=1, source_target_pairs={{1,0},{2,1},{3,2},{4,3},{5,4},{6,5},{7,6},{8,7},{9,8},{10,9},{11,1... | collective-permute-start | bytes 147464 | tf_op jit(solution)/shard_map/ppermute | solution.py:183
  9.5 31.0 %collective-permute-start.6 = (f32[1,128,96]{2,1,0:T(8,128)}, f32[1,128,96]{2,1,0:T(8,128)}, u32[]{:S(2)}, u32[]{:S(2)}) collective-permute-start(f32[1,128,96]{2,1,0:T(8,128)} %bitcast.80), channel_id=1, source_target_pairs={{2,0},{3,1},{4,2},{5,3},{6,4},{7,5},{8,6},{9,7},{10,8},{11,9},{12,... | collective-permute-start | bytes 147464 | tf_op jit(solution)/shard_map/ppermute | solution.py:183
  12.0 31.0 %collective-permute-start.1 = (f32[2,512,48]{1,2,0:T(8,128)S(1)}, f32[2,512,48]{1,2,0:T(8,128)}, u32[]{:S(2)}, u32[]{:S(2)}) collective-permute-start(f32[2,512,48]{1,2,0:T(8,128)S(1)} %copy.48), channel_id=1, source_target_pairs={{0,1},{1,2},{2,3},{3,4},{4,5},{5,6},{6,7},{7,8},{8,9},{9,10},{10,1... | collective-permute-start | bytes 589832 | tf_op jit(solution)/shard_map/ppermute | solution.py:183
  20.9 2.4 %copy-start.16 = (f32[48,48,3,3,3]{1,0,4,3,2:T(8,128)S(1)}, f32[48,48,3,3,3]{1,0,4,3,2:T(8,128)}, u32[]{:S(2)}) copy-start(f32[48,48,3,3,3]{1,0,4,3,2:T(8,128)} %param.16) | copy-start | bytes 746500
  23.4 1.2 %copy-start.17 = (f32[96,48,3,3,3]{0,1,4,3,2:T(8,128)S(1)}, f32[96,48,3,3,3]{0,1,4,3,2:T(8,128)}, u32[]{:S(2)}) copy-start(f32[96,48,3,3,3]{0,1,4,3,2:T(8,128)} %param.24) | copy-start | bytes 1492996
  23.5 1.3 %copy-start.19 = (f32[48,96]{1,0:T(8,128)S(1)}, f32[48,96]{1,0:T(8,128)}, u32[]{:S(2)}) copy-start(f32[48,96]{1,0:T(8,128)} %param.26) | copy-start | bytes 55300
  26.0 3.4 %copy-start.11 = (bf16[9,144,48]{2,1,0:T(8,128)(2,1)S(1)}, bf16[9,144,48]{2,1,0:T(8,128)(2,1)}, u32[]{:S(2)}) copy-start(bf16[9,144,48]{2,1,0:T(8,128)(2,1)} %get-tuple-element.20) | copy-start | bytes 373252
  26.1 3.4 %copy-start.12 = (bf16[9,144,48]{2,1,0:T(8,128)(2,1)S(1)}, bf16[9,144,48]{2,1,0:T(8,128)(2,1)}, u32[]{:S(2)}) copy-start(bf16[9,144,48]{2,1,0:T(8,128)(2,1)} %get-tuple-element.21) | copy-start | bytes 373252
  26.1 3.4 %copy-start.13 = (bf16[9,144,48]{2,1,0:T(8,128)(2,1)S(1)}, bf16[9,144,48]{2,1,0:T(8,128)(2,1)}, u32[]{:S(2)}) copy-start(bf16[9,144,48]{2,1,0:T(8,128)(2,1)} %get-tuple-element.22) | copy-start | bytes 373252
  26.1 3.4 %copy-start.14 = (bf16[9,144,48]{2,1,0:T(8,128)(2,1)S(1)}, bf16[9,144,48]{2,1,0:T(8,128)(2,1)}, u32[]{:S(2)}) copy-start(bf16[9,144,48]{2,1,0:T(8,128)(2,1)} %get-tuple-element.23) | copy-start | bytes 373252
  29.4 1.2 %copy-start.15 = (f32[48,2,16,32]{0,3,2,1:T(8,128)S(1)}, f32[48,2,16,32]{0,3,2,1:T(8,128)}, u32[]{:S(2)}) copy-start(f32[48,2,16,32]{0,3,2,1:T(8,128)} %param.14) | copy-start | bytes 589828
  29.4 10.2 %copy-start.18 = (f32[96,1,8,16]{0,3,2,1:T(8,128)S(1)}, f32[96,1,8,16]{0,3,2,1:T(8,128)}, u32[]{:S(2)}) copy-start(f32[96,1,8,16]{0,3,2,1:T(8,128)} %param.15) | copy-start | bytes 147460
  30.8 12.3 %collective-permute-start.2 = (f32[2,512,48]{1,2,0:T(8,128)S(1)}, f32[2,512,48]{1,2,0:T(8,128)S(1)}, u32[]{:S(2)}, u32[]{:S(2)}) collective-permute-start(f32[2,512,48]{1,2,0:T(8,128)S(1)} %copy.48), channel_id=1, source_target_pairs={{1,0},{2,1},{3,2},{4,3},{5,4},{6,5},{7,6},{8,7},{9,8},{10,9},{11,1... | collective-permute-start | bytes 589832 | tf_op jit(solution)/shard_map/ppermute | solution.py:183
  32.9 10.1 %collective-permute-start = (f32[1,512,48]{1,2,0:T(8,128)S(1)}, f32[1,512,48]{1,2,0:T(8,128)S(1)}, u32[]{:S(2)}, u32[]{:S(2)}) collective-permute-start(f32[1,512,48]{1,2,0:T(8,128)S(1)} %copy.47), channel_id=1, source_target_pairs={{0,2},{1,3},{2,4},{3,5},{4,6},{5,7},{6,8},{7,9},{8,10},{9,11},{10,... | collective-permute-start | bytes 294920 | tf_op jit(solution)/shard_map/ppermute | solution.py:183
  41.3 0.7 copy-start.3
  44.9 1.7 %copy-start.5 = (f32[48]{0:T(128)S(1)}, f32[48]{0:T(128)}, u32[]{:S(2)}) copy-start(f32[48]{0:T(128)} %param.17) | copy-start | bytes 580
  44.9 1.7 %copy-start.6 = (f32[48]{0:T(128)S(1)}, f32[48]{0:T(128)}, u32[]{:S(2)}) copy-start(f32[48]{0:T(128)} %param.19) | copy-start | bytes 580
  44.9 1.7 %copy-start.7 = (f32[96]{0:T(128)S(1)}, f32[96]{0:T(128)}, u32[]{:S(2)}) copy-start(f32[96]{0:T(128)} %param.21) | copy-start | bytes 1156
  44.9 1.8 %copy-start.8 = (f32[96]{0:T(128)S(1)}, f32[96]{0:T(128)}, u32[]{:S(2)}) copy-start(f32[96]{0:T(128)} %param.23) | copy-start | bytes 1156
  44.9 1.8 %copy-start.9 = (f32[96]{0:T(128)S(1)}, f32[96]{0:T(128)}, u32[]{:S(2)}) copy-start(f32[96]{0:T(128)} %param.25) | copy-start | bytes 1156
  44.9 1.8 %copy-start.10 = (f32[48]{0:T(128)S(1)}, f32[48]{0:T(128)}, u32[]{:S(2)}) copy-start(f32[48]{0:T(128)} %param.27) | copy-start | bytes 580
  46.7 1.3 %copy-start = (bf16[9,288,192]{2,1,0:T(8,128)(2,1)S(1)}, bf16[9,288,192]{2,1,0:T(8,128)(2,1)}, u32[]{:S(2)}) copy-start(bf16[9,288,192]{2,1,0:T(8,128)(2,1)} %get-tuple-element.27.wcb) | copy-start | bytes 2985988
  48.0 1.1 %copy-start.1 = (bf16[9,144,192]{2,1,0:T(8,128)(2,1)S(1)}, bf16[9,144,192]{2,1,0:T(8,128)(2,1)}, u32[]{:S(2)}) copy-start(bf16[9,144,192]{2,1,0:T(8,128)(2,1)} %pad_maximum_fusion.3.wd) | copy-start | bytes 1492996
  49.1 1.0 %copy-start.2 = (bf16[9,144,96]{2,1,0:T(8,128)(2,1)S(1)}, bf16[9,144,96]{2,1,0:T(8,128)(2,1)}, u32[]{:S(2)}) copy-start(bf16[9,144,96]{2,1,0:T(8,128)(2,1)} %get-tuple-element.29.wfb) | copy-start | bytes 746500
  50.1 1.0 %copy-start.4 = (f32[5,128,96]{2,1,0:T(8,128)S(1)}, f32[5,128,96]{2,1,0:T(8,128)}, u32[]{:S(2)}) copy-start(f32[5,128,96]{2,1,0:T(8,128)} %copy-done.3) | copy-start | bytes 737284
where the time goes:
time: 91.2 us; the launch traced here: 90.3 us
  Pallas kernels  21.5 us (24%)
  starting transfers between devices  21.4 us (23%)
  local copies, waits for them, and re-layouts  17.9 us (20%)
  blocking collectives  14.7 us (16%)
  other arithmetic  12.9 us (14%)
  waiting for transfers between devices  0.98 us (1%)
  between operations  0.92 us (1%)
    pallas_call x1, Pallas kernels, per_device(): pl.pallas_call(functools.partial(compute, count, width, narrow), out_shap...  21.5 us
    ppermute x7, starting transfers between devices, shifted(): return lax.ppermute(value, 'gx', pairs)  21.4 us
    all_to_all x1, blocking collectives, per_device(): lax.all_to_all(both, 'gx', split_axis=0, concat_axis=0, tiled=True)  14.7 us
    unnamed x46, local copies, waits for them, and re-layouts  8.71 us
    concatenate x3, other arithmetic, split_weights(): return jnp.concatenate([high, moved - high], axis=2).astype(jnp.bfloat16)  5.56 us
    transpose x4, local copies, waits for them, and re-layouts, split_weights(): moved = jnp.transpose(w, (2, 3, 4, 1, 0)).reshape(9, 3 * inner, out)  5.09 us
    another operation x6, other arithmetic  3.26 us
    transpose x1, other arithmetic, per_device(): jnp.transpose(fine_out, (3, 0, 1, 2))  1.92 us
  transfers between devices with their start and end apart: 7, of which 1 were waited for; matrix products, arithmetic and copies ran while one was open for 21% of the time, Pallas kernels for 0%

commit v1 on v0

--- a/solution.py
+++ b/solution.py
@@ -170,6 +170,281 @@
         ][:, :channels]
 
 
+def prepare(raw_ref, out_ref, transposed):
+    def body(t, _):
+        for r in range(3):
+            w = raw_ref[3 * t + r]
+            if transposed:
+                w = w.T
+            high, low = halves(w)
+            inner, out = w.shape
+            out_ref[t, pl.ds(r * inner, inner), pl.ds(0, out)] = high
+            out_ref[t, pl.ds(r * inner, inner), pl.ds(out, out)] = low
+        return 0
+
+    lax.fori_loop(0, 9, body, 0)
+
+
+def joined(
+    count, width, narrow,
+    own, slab, rfa, bfa, rfb, bfb, rca, bca, rcb, bcb, rd, bd, up, bu,
+    fine_ref, coarse_ref,
+    fhi, flo, chi, clo, ftemp, ctemp, mtemp,
+    wfa, wfb, wca, wcb, wd,
+    pair_send, half_send, pair_low, pair_high, half_low, crecv,
+    psend, precv, msend, mrecv, spread,
+    hs, hr, ps, pr, ms, mr,
+):
+    me = lax.axis_index("gx")
+    mesh_id = pl.DeviceIdType.MESH
+    rows, cf = ftemp.shape
+    cc = ctemp.shape[1]
+    levels = ctemp.shape[0] // narrow
+    half = rows // 2
+    barrier = pltpu.get_barrier_semaphore()
+
+    def greet(k, _):
+        pl.semaphore_signal(
+            barrier, inc=1, device_id={"gx": lax.rem(me + k, count)}, device_id_type=mesh_id
+        )
+        return 0
+
+    lax.fori_loop(1, count, greet, 0)
+
+    pair_send[:, pl.ds(0, cf)] = own[0]
+    pair_send[:, pl.ds(cf, cf)] = own[1]
+    half_send[:, pl.ds(0, cf)] = own[1, pl.ds(0, half), :]
+    half_send[:, pl.ds(cf, cf)] = own[1, pl.ds(half, half), :]
+    pl.semaphore_wait(barrier, count - 1)
+
+    halos = (
+        (slab.at[0], crecv.at[1], 1),
+        (slab.at[0], crecv.at[2], -1),
+        (slab.at[0], crecv.at[0], 2),
+        (slab.at[0], crecv.at[3], -2),
+        (pair_send, pair_low, 1),
+        (pair_send, pair_high, -1),
+        (half_send, half_low, 2),
+    )
+
+    def copy_of(k):
+        source, target, step = halos[k]
+        return pltpu.make_async_remote_copy(
+            src_ref=source, dst_ref=target, send_sem=hs.at[k], recv_sem=hr.at[k],
+            device_id={"gx": lax.rem(me + step + count, count)}, device_id_type=mesh_id,
+        )
+
+    def sends(k):
+        step = halos[k][2]
+        return (me + step >= 0) & (me + step < count)
+
+    def receives(k):
+        step = halos[k][2]
+        return (me - step >= 0) & (me - step < count)
+
+    for k in range(7):
+        @pl.when(sends(k))
+        def _():
+            copy_of(k).start()
+
+        @pl.when(jnp.logical_not(receives(k)))
+        def _():
+            target = halos[k][1]
+            target[...] = jnp.zeros(target.shape, jnp.float32)
+
+    prepare(rca, wca, True)
+    prepare(rcb, wcb, True)
+    clear_rims(chi, clo, narrow)
+    clear_rims(fhi, flo, width)
+    put_patches(slab[0], chi, clo, 2, narrow)
+
+    def landed(k):
+        @pl.when(receives(k))
+        def _():
+            copy_of(k).wait_recv()
+
+    for k in range(4):
+        landed(k)
+    for k, slot in enumerate((0, 1, 3, 4)):
+        put_patches(crecv[k], chi, clo, slot, narrow)
+
+    def coarse_mid(j, _):
+        y = me - 1 + j
+        inside = jnp.where((y >= 0) & (y < count), 1.0, 0.0)
+        conv_plane(
+            chi, clo, wca, ctemp, j, narrow,
+            lambda total, at: jnp.maximum(total + bca[...], 0.0) * inside,
+        )
+        put_patches(ctemp[...], chi, clo, j, narrow)
+        return 0
+
+    lax.fori_loop(0, 3, coarse_mid, 0)
+    conv_plane(
+        chi, clo, wcb, ctemp, 0, narrow,
+        lambda total, at: jnp.maximum(slab[0, at, :] + total + bcb[...], 0.0),
+    )
+    uh, ul = halves(up[...].T)
+    projected = product(*halves(ctemp[...]), jnp.concatenate([uh, ul], axis=1)) + bu[...]
+    for d in range(levels):
+        psend[:, d, :] = projected[d * narrow : (d + 1) * narrow]
+
+    def exchange(send, recv, send_sem, recv_sem, k):
+        target = lax.rem(me + k, count)
+        return pltpu.make_async_remote_copy(
+            src_ref=send.at[target], dst_ref=recv.at[me],
+            send_sem=send_sem.at[k], recv_sem=recv_sem.at[k],
+            device_id={"gx": target}, device_id_type=mesh_id,
+        )
+
+    def start_all(send, recv, send_sem, recv_sem):
+        def body(k, _):
+            exchange(send, recv, send_sem, recv_sem, k).start()
+            return 0
+
+        lax.fori_loop(1, count, body, 0)
+        recv[me] = send[me]
+
+    def wait_all(send, recv, send_sem, recv_sem):
+        def body(k, _):
+            source = lax.rem(me - k + count, count)
+            pltpu.make_async_remote_copy(
+                src_ref=send.at[source], dst_ref=recv.at[source],
+                send_sem=send_sem.at[k], recv_sem=recv_sem.at[k],
+                device_id={"gx": source}, device_id_type=mesh_id,
+            ).wait_recv()
+            exchange(send, recv, send_sem, recv_sem, k).wait_send()
+            return 0
+
+        lax.fori_loop(1, count, body, 0)
+
+    start_all(psend, precv, ps, pr)
+
+    prepare(rfa, wfa, True)
+    put_patches(own[0], fhi, flo, 3, width)
+    put_patches(own[1], fhi, flo, 4, width)
+    for k in range(4, 7):
+        landed(k)
+    put_patches(
+        jnp.concatenate([half_low[:, pl.ds(0, cf)], half_low[:, pl.ds(cf, cf)]], axis=0),
+        fhi, flo, 0, width,
+    )
+    put_patches(pair_low[:, pl.ds(0, cf)], fhi, flo, 1, width)
+    put_patches(pair_low[:, pl.ds(cf, cf)], fhi, flo, 2, width)
+    put_patches(pair_high[:, pl.ds(0, cf)], fhi, flo, 5, width)
+    put_patches(pair_high[:, pl.ds(cf, cf)], fhi, flo, 6, width)
+
+    def fine_mid(j, _):
+        x = 2 * me - 2 + j
+        inside = jnp.where((x >= 0) & (x < 2 * count), 1.0, 0.0)
+        conv_plane(
+            fhi, flo, wfa, ftemp, j, width,
+            lambda total, at: jnp.maximum(total + bfa[...], 0.0) * inside,
+        )
+        put_patches(ftemp[...], fhi, flo, j, width)
+        return 0
+
+    lax.fori_loop(0, 5, fine_mid, 0)
+    prepare(rfb, wfb, True)
+    prepare(rd, wd, False)
+    before = jnp.where(me > 0, 1.0, 0.0)
+    conv_plane(
+        fhi, flo, wfb, ftemp, 0, width,
+        lambda total, at: jnp.maximum(pair_low[at, pl.ds(cf, cf)] + total + bfb[...], 0.0) * before,
+    )
+    put_patches(ftemp[...], fhi, flo, 0, width)
+
+    def fine_last(j, _):
+        conv_plane(
+            fhi, flo, wfb, ftemp, j, width,
+            lambda total, at: jnp.maximum(own[j - 1, at, :] + total + bfb[...], 0.0),
+        )
+        put_patches(ftemp[...], fhi, flo, j, width)
+        fine_ref[j - 1] = ftemp[...]
+        return 0
+
+    lax.fori_loop(1, 3, fine_last, 0)
+
+    total = None
+    for p in range(3):
+        for q in range(3):
+            def rows_of(ref):
+                return jnp.concatenate(
+                    [ref[p, pl.ds((2 * b + q) * width, width), :] for b in range(levels)], axis=0
+                )
+            term = product(rows_of(fhi), rows_of(flo), wd[3 * p + q])
+            total = term if total is None else total + term
+    mtemp[:, pl.ds(0, cc)] = total + bd[...]
+    for b in range(levels):
+        msend[:, b, :] = mtemp[pl.ds(b * width, narrow, stride=2), :][:, :cc]
+    start_all(msend, mrecv, ms, mr)
+
+    wait_all(psend, precv, ps, pr)
+    for d in range(rows // width):
+        block = precv[:, d // 2, :]
+        for s in range(2):
+            spread[pl.ds(d * width + s, narrow, stride=2), pl.ds(0, cf)] = block
+    for x in range(2):
+        fine_ref[x] = fine_ref[x] + spread[:, pl.ds(0, cf)]
+    for k in range(7):
+        @pl.when(sends(k))
+        def _():
+            copy_of(k).wait_send()
+
+    wait_all(msend, mrecv, ms, mr)
+    for d in range(levels):
+        at = pl.ds(d * narrow, narrow)
+        coarse_ref[at, :] = ctemp[at, :] + mrecv[:, d, :]
+
+
+def joined_call(count, width, narrow, own, slab, operands):
+    planes, rows, cf = own.shape
+    _, crows, cc = slab.shape
+    levels = crows // narrow
+    f32, bf16 = jnp.float32, jnp.bfloat16
+    vmem = pl.BlockSpec(memory_space=pltpu.VMEM)
+    dma = pltpu.SemaphoreType.DMA
+    return pl.pallas_call(
+        functools.partial(joined, count, width, narrow),
+        out_shape=(
+            jax.ShapeDtypeStruct((planes, rows, cf), f32),
+            jax.ShapeDtypeStruct((crows, cc), f32),
+        ),
+        in_specs=[vmem] * 14,
+        out_specs=(vmem,) * 2,
+        scratch_shapes=[
+            pltpu.VMEM((7, rows + 2 * width, 3 * cf), bf16),
+            pltpu.VMEM((7, rows + 2 * width, 3 * cf), bf16),
+            pltpu.VMEM((5, crows + 2 * narrow, 3 * cc), bf16),
+            pltpu.VMEM((5, crows + 2 * narrow, 3 * cc), bf16),
+            pltpu.VMEM((rows, cf), f32),
+            pltpu.VMEM((crows, cc), f32),
+            pltpu.VMEM((levels * width, 128), f32),
+            pltpu.VMEM((9, 3 * cf, 2 * cf), bf16),
+            pltpu.VMEM((9, 3 * cf, 2 * cf), bf16),
+            pltpu.VMEM((9, 3 * cc, 2 * cc), bf16),
+            pltpu.VMEM((9, 3 * cc, 2 * cc), bf16),
+            pltpu.VMEM((9, 3 * cf, 2 * cc), bf16),
+            pltpu.VMEM((rows, 2 * cf), f32),
+            pltpu.VMEM((rows // 2, 2 * cf), f32),
+            pltpu.VMEM((rows, 2 * cf), f32),
+            pltpu.VMEM((rows, 2 * cf), f32),
+            pltpu.VMEM((rows // 2, 2 * cf), f32),
+            pltpu.VMEM((4, crows, cc), f32),
+            pltpu.VMEM((count, levels, cf), f32),
+            pltpu.VMEM((count, levels, cf), f32),
+            pltpu.VMEM((count, levels, cc), f32),
+            pltpu.VMEM((count, levels, cc), f32),
+            pltpu.VMEM((rows, 128), f32),
+            dma((7,)), dma((7,)),
+            dma((count,)), dma((count,)), dma((count,)), dma((count,)),
+        ],
+        compiler_params=pltpu.CompilerParams(
+            collective_id=0, has_side_effects=True, vmem_limit_bytes=40 * 2**20
+        ),
+        cost_estimate=pl.CostEstimate(flops=10**9, bytes_accessed=6 * 10**6, transcendentals=0),
+    )(own, slab, *operands)
+
+
 def split_weights(w):
     out, inner = w.shape[:2]
     moved = jnp.transpose(w, (2, 3, 4, 1, 0)).reshape(9, 3 * inner, out)
@@ -194,6 +469,27 @@
     cc, _, levels, narrow = coarse_in.shape
     own = jnp.transpose(fine_in, (1, 2, 3, 0)).reshape(planes, depth * width, cf)
     slab = jnp.transpose(coarse_in, (1, 2, 3, 0)).reshape(1, levels * narrow, cc)
+    if depth * width <= ROWS:
+        def taps(w, last):
+            out, inner = w.shape[:2]
+            if last == "in":
+                return jnp.transpose(w, (2, 3, 4, 0, 1)).reshape(27, out, inner)
+            return jnp.transpose(w, (2, 3, 4, 1, 0)).reshape(27, inner, out)
+
+        fine_sum, coarse_sum = joined_call(
+            count, width, narrow, own, slab,
+            (
+                taps(fine_wa, "in"), fine_ba[None], taps(fine_wb, "in"), fine_bb[None],
+                taps(coarse_wa, "in"), coarse_ba[None], taps(coarse_wb, "in"), coarse_bb[None],
+                taps(down_w, "out"), down_b[None], up_w, up_b[None],
+            ),
+        )
+        fine_out = jax.nn.gelu(fine_sum.reshape(planes, depth, width, cf), approximate=False)
+        coarse_out = jax.nn.gelu(coarse_sum.reshape(levels, narrow, cc), approximate=False)
+        return (
+            jnp.transpose(fine_out, (3, 0, 1, 2)),
+            jnp.transpose(coarse_out, (2, 0, 1))[:, None],
+        )
     f7 = jnp.concatenate(
         [shifted(own[1:], 2), shifted(own, 1), own, shifted(own, -1)], axis=0
     )

time: 91.2 us -> 62.1 us (0.68)
  Pallas kernels: 21.5 us -> 45.8 us
  starting transfers between devices: 21.4 us -> 0 us
  blocking collectives: 14.7 us -> 0 us
  other arithmetic: 12.9 us -> 2.72 us
  local copies, waits for them, and re-layouts: 17.9 us -> 12.5 us
  waiting for transfers between devices: 0.98 us -> 0 us
    pallas_call x1, Pallas kernels: 21.5 us -> 45.8 us  [joined_call(): pl.pallas_call(functools.partial(joined, count, width, narrow), out_shape...]
    ppermute x7 -> x0, starting transfers between devices: 21.4 us -> none  [shifted(): return lax.ppermute(value, 'gx', pairs)]
    all_to_all x1 -> x0, blocking collectives: 14.7 us -> none  [per_device(): lax.all_to_all(both, 'gx', split_axis=0, concat_axis=0, tiled=True)]
    concatenate x6 -> x0, other arithmetic: 7.57 us -> none  [the longest x3 5.56 us: split_weights(): return jnp.concatenate([high, moved - high], axis=2).astype(jnp.bfloat16)]
    transpose x6 -> x0, local copies, waits for them, and re-layouts: 5.19 us -> none  [the longest x4 5.09 us: split_weights(): moved = jnp.transpose(w, (2, 3, 4, 1, 0)).reshape(9, 3 * inner, out)]
    unnamed x46 -> x28, local copies, waits for them, and re-layouts: 8.71 us -> 12.5 us
    another operation x6 -> x0, other arithmetic: 3.26 us -> none
    concatenate x2 -> x0, local copies, waits for them, and re-layouts: 2.53 us -> none  [the longest x1 1.69 us: per_device(): jnp.concatenate([shifted(own[1:], 2), shifted(own, 1), own, shifted(own,...]
  transfers between devices with their start and end apart: 7 -> 0, of which waited for: 1 -> 0; matrix products, arithmetic and copies ran while one was open for 21% -> 0% of each run, Pallas kernels for 0% -> 0%
where the time goes in v1:
time: 62.1 us; the launch traced here: 61.6 us
  Pallas kernels  45.8 us (74%)
  local copies, waits for them, and re-layouts  12.5 us (20%)
  other arithmetic  2.72 us (4%)
  between operations  0.68 us (1%)
    pallas_call x1, Pallas kernels, joined_call(): pl.pallas_call(functools.partial(joined, count, width, narrow), out_shape...  45.8 us
    unnamed x28, local copies, waits for them, and re-layouts  12.5 us
    transpose x1, other arithmetic, per_device(): jnp.transpose(fine_out, (3, 0, 1, 2))  1.86 us

profile of v1, /device:TPU:0, one launch (start us, length us, event | category | flops | bytes accessed | tf_op | source)
XLA Modules:
  0.0 61.6 jit_solution(3418169761765556147)
XLA Ops:
  0.6 0.0 copy-start
  0.6 1.3 %copy-done = f32[96,96,3,3,3]{1,0,4,3,2:T(8,128)S(1)} copy-done((f32[96,96,3,3,3]{1,0,4,3,2:T(8,128)S(1)}, f32[96,96,3,3,3]{1,0,4,3,2:T(8,128)}, u32[]{:S(2)}) %copy-start) | copy-done | bytes 995352
  2.0 0.0 copy-start.1
  2.0 1.3 %copy-done.1 = f32[96,96,3,3,3]{1,0,4,3,2:T(8,128)S(1)} copy-done((f32[96,96,3,3,3]{1,0,4,3,2:T(8,128)S(1)}, f32[96,96,3,3,3]{1,0,4,3,2:T(8,128)}, u32[]{:S(2)}) %copy-start.1) | copy-done | bytes 995352
  3.3 0.0 copy-start.2
  3.3 1.1 %copy-done.2 = f32[48,48,3,3,3]{1,0,4,3,2:T(8,128)S(1)} copy-done((f32[48,48,3,3,3]{1,0,4,3,2:T(8,128)S(1)}, f32[48,48,3,3,3]{1,0,4,3,2:T(8,128)}, u32[]{:S(2)}) %copy-start.2) | copy-done | bytes 248856
  4.4 0.0 copy-start.3
  4.4 1.1 %copy-done.3 = f32[48,48,3,3,3]{1,0,4,3,2:T(8,128)S(1)} copy-done((f32[48,48,3,3,3]{1,0,4,3,2:T(8,128)S(1)}, f32[48,48,3,3,3]{1,0,4,3,2:T(8,128)}, u32[]{:S(2)}) %copy-start.3) | copy-done | bytes 248856
  5.5 0.0 copy-start.4
  5.5 1.1 %copy-done.4 = f32[96,48,3,3,3]{0,1,4,3,2:T(8,128)S(1)} copy-done((f32[96,48,3,3,3]{0,1,4,3,2:T(8,128)S(1)}, f32[96,48,3,3,3]{0,1,4,3,2:T(8,128)}, u32[]{:S(2)}) %copy-start.4) | copy-done | bytes 497688
  6.6 0.0 copy-start.5
  6.6 1.0 %copy-done.5 = f32[48,2,16,32]{0,3,2,1:T(8,128)S(1)} copy-done((f32[48,2,16,32]{0,3,2,1:T(8,128)S(1)}, f32[48,2,16,32]{0,3,2,1:T(8,128)}, u32[]{:S(2)}) %copy-start.5) | copy-done | bytes 196632
  7.6 0.0 copy-start.6
  7.6 0.8 %copy-done.6 = f32[96,1,8,16]{0,3,2,1:T(8,128)S(1)} copy-done((f32[96,1,8,16]{0,3,2,1:T(8,128)S(1)}, f32[96,1,8,16]{0,3,2,1:T(8,128)}, u32[]{:S(2)}) %copy-start.6) | copy-done | bytes 49176
  8.4 0.0 copy-start.7
  8.4 0.7 %copy-done.7 = f32[48,96]{1,0:T(8,128)S(1)} copy-done((f32[48,96]{1,0:T(8,128)S(1)}, f32[48,96]{1,0:T(8,128)}, u32[]{:S(2)}) %copy-start.7) | copy-done | bytes 18456
  9.2 0.0 copy-start.8
  9.2 0.7 %copy-done.8 = f32[48]{0:T(128)S(1)} copy-done((f32[48]{0:T(128)S(1)}, f32[48]{0:T(128)}, u32[]{:S(2)}) %copy-start.8) | copy-done | bytes 216
  9.8 0.0 copy-start.9
  9.8 0.7 %copy-done.9 = f32[48]{0:T(128)S(1)} copy-done((f32[48]{0:T(128)S(1)}, f32[48]{0:T(128)}, u32[]{:S(2)}) %copy-start.9) | copy-done | bytes 216
  10.5 0.0 copy-start.10
  10.5 0.7 %copy-done.10 = f32[96]{0:T(128)S(1)} copy-done((f32[96]{0:T(128)S(1)}, f32[96]{0:T(128)}, u32[]{:S(2)}) %copy-start.10) | copy-done | bytes 408
  11.1 0.0 copy-start.11
  11.1 0.7 %copy-done.11 = f32[96]{0:T(128)S(1)} copy-done((f32[96]{0:T(128)S(1)}, f32[96]{0:T(128)}, u32[]{:S(2)}) %copy-start.11) | copy-done | bytes 408
  11.8 0.0 copy-start.12
  11.8 0.7 %copy-done.12 = f32[96]{0:T(128)S(1)} copy-done((f32[96]{0:T(128)S(1)}, f32[96]{0:T(128)}, u32[]{:S(2)}) %copy-start.12) | copy-done | bytes 408
  12.5 0.0 copy-start.13
  12.5 0.7 %copy-done.13 = f32[48]{0:T(128)S(1)} copy-done((f32[48]{0:T(128)S(1)}, f32[48]{0:T(128)}, u32[]{:S(2)}) %copy-start.13) | copy-done | bytes 216
  13.1 45.8 %shard_map.149 = (f32[2,512,48]{2,1,0:T(8,128)S(1)}, f32[128,96]{1,0:T(8,128)S(1)}) custom-call(f32[2,512,48]{2,1,0:T(8,128)S(1)} %bitcast.42, f32[1,128,96]{2,1,0:T(8,128)S(1)} %bitcast.43, f32[27,48,48]{2,1,0:T(8,128)S(1)} %bitcast.39, f32[1,48]{1,0:T(1,128)S(1)} %bitcast.44, f32[27,48,48]{2,1,0:T(8,128)S(1)} %bitcast.40, f32[1,48]{1,0:T(1,128)S(1)} %bitcast.45, ...), custom_call_target="tpu_custom_call" | custom-call | flops 1000000000 | bytes 6000000 | tf_op jit(solution)/shard_map/pallas_call | solution.py:406
  58.9 0.8 %fusion.11 = f32[96,1,8,16]{0,3,2,1:T(8,128)} fusion(f32[8,16,96]{2,1,0:T(8,128)S(1)} %bitcast.53, f32[8,16,96]{2,1,0:T(8,128)S(1)} %bitcast.52), kind=kLoop, calls=%fused_computation.22 | loop fusion | flops 749568 | bytes 147456 | tf_op jit(solution)/shard_map/broadcast_in_dim | solution.py:491
  59.7 0.1 negate_multiply_fusion
  59.8 1.9 %fusion.2 = f32[48,2,16,32]{0,3,2,1:T(8,128)} fusion(f32[2,16,32,48]{3,2,1,0:T(8,128)S(1)} %bitcast.51, f32[2,16,32,48]{3,2,1,0:T(8,128)S(1)} %bitcast.50), kind=kLoop, calls=%fused_computation.3 | loop fusion | flops 2998272 | bytes 589824 | tf_op jit(solution)/shard_map/transpose | solution.py:490
  (1 shorter events, 0.0 us)
Async XLA Ops:
  0.6 1.3 %copy-start = (f32[96,96,3,3,3]{1,0,4,3,2:T(8,128)S(1)}, f32[96,96,3,3,3]{1,0,4,3,2:T(8,128)}, u32[]{:S(2)}) copy-start(f32[96,96,3,3,3]{1,0,4,3,2:T(8,128)} %param.20) | copy-start | bytes 2985988
  2.0 1.3 %copy-start.1 = (f32[96,96,3,3,3]{1,0,4,3,2:T(8,128)S(1)}, f32[96,96,3,3,3]{1,0,4,3,2:T(8,128)}, u32[]{:S(2)}) copy-start(f32[96,96,3,3,3]{1,0,4,3,2:T(8,128)} %param.22) | copy-start | bytes 2985988
  3.3 1.1 %copy-start.2 = (f32[48,48,3,3,3]{1,0,4,3,2:T(8,128)S(1)}, f32[48,48,3,3,3]{1,0,4,3,2:T(8,128)}, u32[]{:S(2)}) copy-start(f32[48,48,3,3,3]{1,0,4,3,2:T(8,128)} %param.16) | copy-start | bytes 746500
  4.4 1.1 %copy-start.3 = (f32[48,48,3,3,3]{1,0,4,3,2:T(8,128)S(1)}, f32[48,48,3,3,3]{1,0,4,3,2:T(8,128)}, u32[]{:S(2)}) copy-start(f32[48,48,3,3,3]{1,0,4,3,2:T(8,128)} %param.18) | copy-start | bytes 746500
  5.5 1.1 %copy-start.4 = (f32[96,48,3,3,3]{0,1,4,3,2:T(8,128)S(1)}, f32[96,48,3,3,3]{0,1,4,3,2:T(8,128)}, u32[]{:S(2)}) copy-start(f32[96,48,3,3,3]{0,1,4,3,2:T(8,128)} %param.24) | copy-start | bytes 1492996
  6.6 1.0 %copy-start.5 = (f32[48,2,16,32]{0,3,2,1:T(8,128)S(1)}, f32[48,2,16,32]{0,3,2,1:T(8,128)}, u32[]{:S(2)}) copy-start(f32[48,2,16,32]{0,3,2,1:T(8,128)} %param.14) | copy-start | bytes 589828
  7.6 0.8 %copy-start.6 = (f32[96,1,8,16]{0,3,2,1:T(8,128)S(1)}, f32[96,1,8,16]{0,3,2,1:T(8,128)}, u32[]{:S(2)}) copy-start(f32[96,1,8,16]{0,3,2,1:T(8,128)} %param.15) | copy-start | bytes 147460
  8.4 0.7 %copy-start.7 = (f32[48,96]{1,0:T(8,128)S(1)}, f32[48,96]{1,0:T(8,128)}, u32[]{:S(2)}) copy-start(f32[48,96]{1,0:T(8,128)} %up.1) | copy-start | bytes 55300
  9.2 0.7 %copy-start.8 = (f32[48]{0:T(128)S(1)}, f32[48]{0:T(128)}, u32[]{:S(2)}) copy-start(f32[48]{0:T(128)} %param.17) | copy-start | bytes 580
  9.8 0.7 %copy-start.9 = (f32[48]{0:T(128)S(1)}, f32[48]{0:T(128)}, u32[]{:S(2)}) copy-start(f32[48]{0:T(128)} %param.19) | copy-start | bytes 580
  10.5 0.7 %copy-start.10 = (f32[96]{0:T(128)S(1)}, f32[96]{0:T(128)}, u32[]{:S(2)}) copy-start(f32[96]{0:T(128)} %param.21) | copy-start | bytes 1156
  11.1 0.7 %copy-start.11 = (f32[96]{0:T(128)S(1)}, f32[96]{0:T(128)}, u32[]{:S(2)}) copy-start(f32[96]{0:T(128)} %param.23) | copy-start | bytes 1156
  11.8 0.7 %copy-start.12 = (f32[96]{0:T(128)S(1)}, f32[96]{0:T(128)}, u32[]{:S(2)}) copy-start(f32[96]{0:T(128)} %param.25) | copy-start | bytes 1156
  12.5 0.7 %copy-start.13 = (f32[48]{0:T(128)S(1)}, f32[48]{0:T(128)}, u32[]{:S(2)}) copy-start(f32[48]{0:T(128)} %param.27) | copy-start | bytes 580

commit v2 on v1

--- a/solution.py
+++ b/solution.py
@@ -35,11 +35,25 @@
         ref[:, pl.ds(rows - width, width), :] = zero
 
 
-def product(high, low, weights):
+def terms(high, low, weights):
     out = weights.shape[1] // 2
     both = jnp.dot(high, weights, preferred_element_type=jnp.float32)
     third = jnp.dot(low, weights[:, :out], preferred_element_type=jnp.float32)
+    return both, third
+
+
+def added(total, pair):
+    return pair if total is None else (total[0] + pair[0], total[1] + pair[1])
+
+
+def folded(pair):
+    both, third = pair
+    out = third.shape[1]
     return both[:, :out] + both[:, out:] + third
+
+
+def product(high, low, weights):
+    return folded(terms(high, low, weights))
 
 
 def conv_chunk(high_ref, low_ref, w_ref, slot, start, rows, width):
@@ -47,9 +61,11 @@
     for p in range(3):
         for q in range(3):
             at = pl.ds(pl.multiple_of(start + q * width, 16), rows)
-            term = product(high_ref[slot + p, at, :], low_ref[slot + p, at, :], w_ref[3 * p + q])
-            total = term if total is None else total + term
-    return total
+            total = added(
+                total,
+                terms(high_ref[slot + p, at, :], low_ref[slot + p, at, :], w_ref[3 * p + q]),
+            )
+    return folded(total)
 
 
 def conv_plane(high_ref, low_ref, w_ref, temp_ref, slot, width, finish):
@@ -161,8 +177,8 @@
                         [ref[p, pl.ds((2 * b + q) * width, width), :] for b in range(first, first + some)],
                         axis=0,
                     )
-                term = product(rows_of(fhi), rows_of(flo), wd[3 * p + q])
-                total = term if total is None else total + term
+                total = added(total, terms(rows_of(fhi), rows_of(flo), wd[3 * p + q]))
+        total = folded(total)
         channels = total.shape[1]
         mtemp[:, pl.ds(0, channels)] = total + bd[...]
         moved_ref[pl.ds(first * narrow, some * narrow), :] = mtemp[
@@ -187,14 +203,26 @@
 
 def joined(
     count, width, narrow,
-    own, slab, rfa, bfa, rfb, bfb, rca, bca, rcb, bcb, rd, bd, up, bu,
-    fine_ref, coarse_ref,
+    *refs,
+):
+    sources, (fine_ref, coarse_ref) = refs[:14], refs[14:16]
+    local, fetched = refs[16:30], refs[30]
+    joined_body(count, width, narrow, sources, local, fetched, fine_ref, coarse_ref, *refs[31:])
+
+
+def joined_body(
+    count, width, narrow, sources, local, fetched, fine_ref, coarse_ref,
     fhi, flo, chi, clo, ftemp, ctemp, mtemp,
     wfa, wfb, wca, wcb, wd,
     pair_send, half_send, pair_low, pair_high, half_low, crecv,
     psend, precv, msend, mrecv, spread,
     hs, hr, ps, pr, ms, mr,
 ):
+    own, slab, rfa, bfa, rfb, bfb, rca, bca, rcb, bcb, rd, bd, up, bu = local
+
+    def fetch(k):
+        return pltpu.make_async_copy(sources[k], local[k], fetched.at[k])
+
     me = lax.axis_index("gx")
     mesh_id = pl.DeviceIdType.MESH
     rows, cf = ftemp.shape
@@ -210,6 +238,10 @@
         return 0
 
     lax.fori_loop(1, count, greet, 0)
+    for k in (1, 0, 6, 7, 8, 9, 2, 3, 12, 13, 4, 5, 10, 11):
+        fetch(k).start()
+    fetch(1).wait()
+    fetch(0).wait()
 
     pair_send[:, pl.ds(0, cf)] = own[0]
     pair_send[:, pl.ds(cf, cf)] = own[1]
@@ -252,10 +284,12 @@
             target = halos[k][1]
             target[...] = jnp.zeros(target.shape, jnp.float32)
 
+    clear_rims(chi, clo, narrow)
+    clear_rims(fhi, flo, width)
+    for k in range(2, 14):
+        fetch(k).wait()
     prepare(rca, wca, True)
     prepare(rcb, wcb, True)
-    clear_rims(chi, clo, narrow)
-    clear_rims(fhi, flo, width)
     put_patches(slab[0], chi, clo, 2, narrow)
 
     def landed(k):
@@ -371,8 +405,8 @@
                 return jnp.concatenate(
                     [ref[p, pl.ds((2 * b + q) * width, width), :] for b in range(levels)], axis=0
                 )
-            term = product(rows_of(fhi), rows_of(flo), wd[3 * p + q])
-            total = term if total is None else total + term
+            total = added(total, terms(rows_of(fhi), rows_of(flo), wd[3 * p + q]))
+    total = folded(total)
     mtemp[:, pl.ds(0, cc)] = total + bd[...]
     for b in range(levels):
         msend[:, b, :] = mtemp[pl.ds(b * width, narrow, stride=2), :][:, :cc]
@@ -409,9 +443,11 @@
             jax.ShapeDtypeStruct((planes, rows, cf), f32),
             jax.ShapeDtypeStruct((crows, cc), f32),
         ),
-        in_specs=[vmem] * 14,
+        in_specs=[pl.BlockSpec(memory_space=pl.ANY)] * 14,
         out_specs=(vmem,) * 2,
-        scratch_shapes=[
+        scratch_shapes=[pltpu.VMEM(v.shape, f32) for v in (own, slab) + operands]
+        + [
+            dma((14,)),
             pltpu.VMEM((7, rows + 2 * width, 3 * cf), bf16),
             pltpu.VMEM((7, rows + 2 * width, 3 * cf), bf16),
             pltpu.VMEM((5, crows + 2 * narrow, 3 * cc), bf16),
@@ -439,7 +475,7 @@
             dma((count,)), dma((count,)), dma((count,)), dma((count,)),
         ],
         compiler_params=pltpu.CompilerParams(
-            collective_id=0, has_side_effects=True, vmem_limit_bytes=40 * 2**20
+            collective_id=0, has_side_effects=True, vmem_limit_bytes=60 * 2**20
         ),
         cost_estimate=pl.CostEstimate(flops=10**9, bytes_accessed=6 * 10**6, transcendentals=0),
     )(own, slab, *operands)

time: 62.1 us -> 52.5 us (0.85)
  local copies, waits for them, and re-layouts: 12.5 us -> 0 us
  other arithmetic: 2.72 us -> 4.6 us
  Pallas kernels: 45.8 us -> 47 us
    unnamed x28 -> x0, local copies, waits for them, and re-layouts: 12.5 us -> none
    pallas_call x1, Pallas kernels: 45.8 us -> 47 us  [joined_call(): pl.pallas_call(functools.partial(joined, count, width, narrow), out_shape...]
    mul x1, other arithmetic: 0.07 us -> 1.11 us  [per_device(): jax.nn.gelu(fine_sum.reshape(planes, depth, width, cf), approximate=False)]
    mul x1, other arithmetic: 0.01 us -> 0.85 us  [per_device(): jax.nn.gelu(coarse_sum.reshape(levels, narrow, cc), approximate=False)]
where the time goes in v2:
time: 52.5 us; the launch traced here: 52.3 us
  Pallas kernels  47 us (90%)
  other arithmetic  4.6 us (9%)
  between operations  0.65 us (1%)
    pallas_call x1, Pallas kernels, joined_call(): pl.pallas_call(functools.partial(joined, count, width, narrow), out_shape...  47 us
    transpose x1, other arithmetic, per_device(): jnp.transpose(fine_out, (3, 0, 1, 2))  1.86 us
    mul x1, other arithmetic, per_device(): jax.nn.gelu(fine_sum.reshape(planes, depth, width, cf), approximate=False)  1.11 us

profile of v2, /device:TPU:0, one launch (start us, length us, event | category | flops | bytes accessed | tf_op | source)
XLA Modules:
  0.0 52.3 jit_solution(18262570512135723795)
XLA Ops:
  0.6 47.0 %shard_map.149 = (f32[2,512,48]{2,1,0:T(8,128)}, f32[128,96]{1,0:T(8,128)}) custom-call(f32[2,512,48]{2,1,0:T(8,128)} %bitcast.44, f32[1,128,96]{2,1,0:T(8,128)} %bitcast.47, f32[27,48,48]{2,1,0:T(8,128)} %bitcast.41, f32[1,48]{1,0:T(1,128)} %bitcast.48, f32[27,48,48]{2,1,0:T(8,128)} %bitcast.42, f32[1,48]{1,0:T(1,128)} %bitcast.49, f32[27,96,96]{2,1,0:T(8,128)} %bitcast.39, ...), custom_call_target="tpu_custom_call" | custom-call | flops 1000000000 | bytes 6000000 | tf_op jit(solution)/shard_map/pallas_call | solution.py:440
  47.7 0.9 %negate_multiply_fusion.1 = (f32[128,96]{1,0:T(8,128)S(1)}, f32[128,96]{1,0:T(8,128)S(1)}) fusion(f32[128,96]{1,0:T(8,128)} %get-tuple-element.5), kind=kLoop, calls=%fused_computation.35 | loop fusion | flops 36864 | bytes 147456 | tf_op jit(solution)/shard_map/mul | solution.py:524
  48.5 0.8 %fusion.11 = f32[96,1,8,16]{0,3,2,1:T(8,128)} fusion(f32[8,16,96]{2,1,0:T(8,128)S(1)} %bitcast.46, f32[8,16,96]{2,1,0:T(8,128)S(1)} %bitcast.45), kind=kLoop, calls=%fused_computation.22 | loop fusion | flops 749568 | bytes 147456 | tf_op jit(solution)/shard_map/broadcast_in_dim | solution.py:527
  49.3 1.1 %negate_multiply_fusion = (f32[2,512,48]{2,1,0:T(8,128)S(1)}, f32[2,512,48]{2,1,0:T(8,128)S(1)}) fusion(f32[2,512,48]{2,1,0:T(8,128)} %get-tuple-element.4), kind=kLoop, calls=%fused_computation.16 | loop fusion | flops 147456 | bytes 589824 | tf_op jit(solution)/shard_map/mul | solution.py:523
  50.4 1.9 %fusion.2 = f32[48,2,16,32]{0,3,2,1:T(8,128)} fusion(f32[2,16,32,48]{3,2,1,0:T(8,128)S(1)} %bitcast.38, f32[2,16,32,48]{3,2,1,0:T(8,128)S(1)} %bitcast.37), kind=kLoop, calls=%fused_computation.3 | loop fusion | flops 2998272 | bytes 589824 | tf_op jit(solution)/shard_map/transpose | solution.py:526

commit v3 on v2

--- a/solution.py
+++ b/solution.py
@@ -292,6 +292,12 @@
     prepare(rcb, wcb, True)
     put_patches(slab[0], chi, clo, 2, narrow)
 
+    prepare(rfa, wfa, True)
+    prepare(rfb, wfb, True)
+    prepare(rd, wd, False)
+    put_patches(own[0], fhi, flo, 3, width)
+    put_patches(own[1], fhi, flo, 4, width)
+
     def landed(k):
         @pl.when(receives(k))
         def _():
@@ -353,9 +359,6 @@
 
     start_all(psend, precv, ps, pr)
 
-    prepare(rfa, wfa, True)
-    put_patches(own[0], fhi, flo, 3, width)
-    put_patches(own[1], fhi, flo, 4, width)
     for k in range(4, 7):
         landed(k)
     put_patches(
@@ -378,8 +381,6 @@
         return 0
 
     lax.fori_loop(0, 5, fine_mid, 0)
-    prepare(rfb, wfb, True)
-    prepare(rd, wd, False)
     before = jnp.where(me > 0, 1.0, 0.0)
     conv_plane(
         fhi, flo, wfb, ftemp, 0, width,

time: 52.5 us -> 47.9 us (0.912)
  Pallas kernels: 47 us -> 42.5 us
    pallas_call x1, Pallas kernels: 47 us -> 42.5 us  [joined_call(): pl.pallas_call(functools.partial(joined, count, width, narrow), out_shape...]
where the time goes in v3:
time: 47.9 us; the launch traced here: 47.7 us
  Pallas kernels  42.5 us (89%)
  other arithmetic  4.6 us (10%)
  between operations  0.65 us (1%)
    pallas_call x1, Pallas kernels, joined_call(): pl.pallas_call(functools.partial(joined, count, width, narrow), out_shape...  42.5 us
    transpose x1, other arithmetic, per_device(): jnp.transpose(fine_out, (3, 0, 1, 2))  1.86 us
    mul x1, other arithmetic, per_device(): jax.nn.gelu(fine_sum.reshape(planes, depth, width, cf), approximate=False)  1.11 us

profile of v3, /device:TPU:0, one launch (start us, length us, event | category | flops | bytes accessed | tf_op | source)
XLA Modules:
  0.0 47.7 jit_solution(14783238451364586154)
XLA Ops:
  0.6 42.5 %shard_map.149 = (f32[2,512,48]{2,1,0:T(8,128)}, f32[128,96]{1,0:T(8,128)}) custom-call(f32[2,512,48]{2,1,0:T(8,128)} %bitcast.44, f32[1,128,96]{2,1,0:T(8,128)} %bitcast.47, f32[27,48,48]{2,1,0:T(8,128)} %bitcast.41, f32[1,48]{1,0:T(1,128)} %bitcast.48, f32[27,48,48]{2,1,0:T(8,128)} %bitcast.42, f32[1,48]{1,0:T(1,128)} %bitcast.49, f32[27,96,96]{2,1,0:T(8,128)} %bitcast.39, ...), custom_call_target="tpu_custom_call" | custom-call | flops 1000000000 | bytes 6000000 | tf_op jit(solution)/shard_map/pallas_call | solution.py:441
  43.1 0.9 %negate_multiply_fusion.1 = (f32[128,96]{1,0:T(8,128)S(1)}, f32[128,96]{1,0:T(8,128)S(1)}) fusion(f32[128,96]{1,0:T(8,128)} %get-tuple-element.5), kind=kLoop, calls=%fused_computation.35 | loop fusion | flops 36864 | bytes 147456 | tf_op jit(solution)/shard_map/mul | solution.py:525
  44.0 0.8 %fusion.11 = f32[96,1,8,16]{0,3,2,1:T(8,128)} fusion(f32[8,16,96]{2,1,0:T(8,128)S(1)} %bitcast.46, f32[8,16,96]{2,1,0:T(8,128)S(1)} %bitcast.45), kind=kLoop, calls=%fused_computation.22 | loop fusion | flops 749568 | bytes 147456 | tf_op jit(solution)/shard_map/broadcast_in_dim | solution.py:528
  44.7 1.1 %negate_multiply_fusion = (f32[2,512,48]{2,1,0:T(8,128)S(1)}, f32[2,512,48]{2,1,0:T(8,128)S(1)}) fusion(f32[2,512,48]{2,1,0:T(8,128)} %get-tuple-element.4), kind=kLoop, calls=%fused_computation.16 | loop fusion | flops 147456 | bytes 589824 | tf_op jit(solution)/shard_map/mul | solution.py:524
  45.9 1.9 %fusion.2 = f32[48,2,16,32]{0,3,2,1:T(8,128)} fusion(f32[2,16,32,48]{3,2,1,0:T(8,128)S(1)} %bitcast.38, f32[2,16,32,48]{3,2,1,0:T(8,128)S(1)} %bitcast.37), kind=kLoop, calls=%fused_computation.3 | loop fusion | flops 2998272 | bytes 589824 | tf_op jit(solution)/shard_map/transpose | solution.py:527
